TPU v7x, 256 devices: a whole 4x4x8 slice. The times are simulated.
256 devices in a mesh: row: 4 (over y), col: 16 (over z, core), layer: 4 (over x).
Axes of the slice: x: 4, y: 4, z: 8, core: 2. Of those that a mesh axis runs over, the one named last changes fastest.
Arguments:
- density: float32 [4096, 4096], P('row', 'col'), may hold values from -1 to 1, as said below
- pattern: int32 [64, 64], replicated, may hold values from 0 to 1, as said below
Outputs:
- purified: float32 [4096, 4096], P('row', 'col')
- traces: float32 [2], replicated
Inputs may be any that keep to these rules, and one draw needn't show every extreme that they name: pattern is symmetric and is 1 on the block diagonal and next to it. density is symmetric and zero outside the blocks that pattern keeps.
All inputs are finite; a program needn't handle non-finite values.
Results may differ from a plain program's by a relative error of at most 0.0003.
Values sent between devices are 32-bit elements; how exact they have to be, the bound alone decides.
No kernel may reach another device: no remote copies, remote signals or barrier semaphores. Data moves between devices by JAX's collectives and lax.ppermute only.
A program may use at most 64 MiB of HBM per device.

v0:
```python
import jax
import jax.numpy as jnp
from jax import lax
from jax.sharding import PartitionSpec as P

BS = 64
STEPS = 2
HIGHEST = lax.Precision.HIGHEST


def pick_columns(tile, layer_index, unit_width, layers):
    tile_rows, tile_cols = tile.shape
    shaped = tile.reshape(tile_rows, tile_cols // (layers * unit_width), layers, unit_width)
    picked = lax.dynamic_index_in_dim(shaped, layer_index, 2, keepdims=False)
    return picked.reshape(tile_rows, tile_cols // layers)


def pick_rows(tile, layer_index, unit_width, layers):
    tile_rows, tile_cols = tile.shape
    shaped = tile.reshape(tile_rows // (layers * unit_width), layers, unit_width, tile_cols)
    picked = lax.dynamic_index_in_dim(shaped, layer_index, 1, keepdims=False)
    return picked.reshape(tile_rows // layers, tile_cols)


def reduce_layers(layer_term):
    summed = lax.psum(layer_term, "layer")
    return summed


def right_panel(right, layer_index, unit_width, layers):
    return lax.all_gather(
        pick_rows(right, layer_index, unit_width, layers), "row", axis=0, tiled=True
    )


def folded_product(left, right, layer_index, unit_width, layers, occupied):
    tall_panel = right_panel(right, layer_index, unit_width, layers)
    layer_term = jnp.dot(
        lax.all_gather(
            pick_columns(left, layer_index, unit_width, layers), "col", axis=1, tiled=True
        ),
        tall_panel,
        precision=HIGHEST,
        preferred_element_type=jnp.float32,
    )
    summed = reduce_layers(layer_term)
    return jnp.where(occupied, summed, jnp.zeros_like(summed))


def body(density, pattern):
    tile_rows, tile_cols = density.shape
    layers = lax.axis_size("layer")
    unit_width = tile_cols // (lax.axis_size("row") * layers)
    layer_index = lax.axis_index("layer")
    row_ids = lax.axis_index("row") * tile_rows + jnp.arange(tile_rows, dtype=jnp.int32)
    col_ids = lax.axis_index("col") * tile_cols + jnp.arange(tile_cols, dtype=jnp.int32)
    blocks = jnp.arange(pattern.shape[0], dtype=jnp.int32)
    row_onehot = (row_ids[:, None] // BS == blocks[None, :]).astype(jnp.bfloat16)
    col_onehot = (blocks[:, None] == col_ids[None, :] // BS).astype(jnp.bfloat16)
    row_pattern = jnp.dot(
        row_onehot, pattern.astype(jnp.bfloat16), preferred_element_type=jnp.float32
    )
    occupied = (
        jnp.dot(row_pattern.astype(jnp.bfloat16), col_onehot, preferred_element_type=jnp.float32)
        > 0.5
    )
    on_diag = row_ids[:, None] == col_ids[None, :]
    current = density
    trace_list = []
    for iteration in range(STEPS):
        square = folded_product(current, current, layer_index, unit_width, layers, occupied)
        cube_term = folded_product(current, square, layer_index, unit_width, layers, occupied)
        current = 3.0 * square - 2.0 * cube_term
        diag_part = jnp.sum(jnp.where(on_diag, current, jnp.zeros_like(current)))
        trace_list.append(lax.psum(diag_part, ("row", "col")))
    stacked = jnp.stack(trace_list)
    return (current, stacked)


def solution(mesh):
    placed = (P("row", "col"), P())
    return jax.shard_map(
        body, mesh=mesh, in_specs=placed, out_specs=(P("row", "col"), P()), check_vma=False
    )
```

profile of v0, /device:TPU:2, one launch (start us, length us, event | category | flops | bytes accessed | tf_op | source)
XLA Modules:
  0.0 601.4 jit_solution(12206215405275679510)
XLA Ops:
  7.2 1.7 constant_dynamic-slice_fusion.4
  9.0 1.6 copy.4
  11.4 28.0 %all-gather.9.cloned.1.call-done = f32[1024,256]{1,0:T(8,128)} async-done(((f32[256,256]{1,0:T(8,128)}), f32[1024,256]{1,0:T(8,128)}) %all-gather.9.cloned.1.call-update) | async-done | bytes 1048592 | tf_op jit(solution)/shard_map/all_gather | solution.py:31
  39.3 44.9 %all-gather.7.cloned.1.call-done = f32[1024,1024]{0,1:T(8,128)} async-done(((f32[1024,64]{0,1:T(8,128)}), f32[1024,1024]{0,1:T(8,128)}) %all-gather.7.cloned.1.call-update) | async-done | bytes 4194320 | tf_op jit(solution)/shard_map/all_gather | solution.py:39
  84.2 10.1 %fusion.12 = f32[1024,256]{1,0:T(8,128)} fusion(f32[1024,1024]{0,1:T(8,128)} %all-gather.7.cloned.1.call-done, f32[1024,256]{1,0:T(8,128)} %all-gather.9.cloned.1.call-done), kind=kOutput, calls=%fused_computation.36 | convolution fusion | flops 3221225472 | bytes 6291456 | tf_op jit(solution)/shard_map/dot_general | solution.py:38
  94.4 48.7 %all-reduce.6.cloned.1.call-done = f32[1024,256]{1,0:T(8,128)} async-done(((f32[1024,256]{1,0:T(8,128)}), f32[1024,256]{1,0:T(8,128)}) %all-reduce.6.cloned.1.call-update) | async-done | bytes 1048592 | tf_op jit(solution)/shard_map/psum | solution.py:26
  143.2 1.8 broadcast_select_fusion.1
  145.0 0.7 constant_dynamic-slice_fusion.3
  146.0 28.2 %all-gather.11.cloned.1.call-done = f32[1024,256]{1,0:T(8,128)} async-done(((f32[256,256]{1,0:T(8,128)}), f32[1024,256]{1,0:T(8,128)}) %all-gather.11.cloned.1.call-update) | async-done | bytes 1048592 | tf_op jit(solution)/shard_map/all_gather | solution.py:31
  174.1 10.1 %fusion.13 = f32[1024,256]{1,0:T(8,128)} fusion(f32[1024,1024]{0,1:T(8,128)} %all-gather.7.cloned.1.call-done, f32[1024,256]{1,0:T(8,128)} %all-gather.11.cloned.1.call-done), kind=kOutput, calls=%fused_computation.37 | convolution fusion | flops 3221225472 | bytes 6291456 | tf_op jit(solution)/shard_map/dot_general | solution.py:38
  184.3 50.6 %all-reduce.8.cloned.1.call-done = f32[1024,256]{1,0:T(8,128)} async-done(((f32[1024,256]{1,0:T(8,128)}), f32[1024,256]{1,0:T(8,128)}) %all-reduce.8.cloned.1.call-update) | async-done | bytes 1048592 | tf_op jit(solution)/shard_map/psum | solution.py:26
  234.9 1.5 multiply_subtract_fusion.1
  236.3 0.8 constant_dynamic-slice_fusion.1
  238.5 27.0 %all-gather.15.cloned.1.call-done = f32[1024,256]{1,0:T(8,128)} async-done(((f32[256,256]{1,0:T(8,128)}), f32[1024,256]{1,0:T(8,128)}) %all-gather.15.cloned.1.call-update) | async-done | bytes 1048592 | tf_op jit(solution)/shard_map/all_gather | solution.py:31
  265.5 44.9 %all-gather.13.cloned.1.call-done = f32[1024,1024]{0,1:T(8,128)} async-done(((f32[1024,64]{0,1:T(8,128)}), f32[1024,1024]{0,1:T(8,128)}) %all-gather.13.cloned.1.call-update) | async-done | bytes 4194320 | tf_op jit(solution)/shard_map/all_gather | solution.py:39
  310.4 10.1 %fusion.14 = f32[1024,256]{1,0:T(8,128)} fusion(f32[1024,1024]{0,1:T(8,128)} %all-gather.13.cloned.1.call-done, f32[1024,256]{1,0:T(8,128)} %all-gather.15.cloned.1.call-done), kind=kOutput, calls=%fused_computation.38 | convolution fusion | flops 3221225472 | bytes 6291456 | tf_op jit(solution)/shard_map/dot_general | solution.py:38
  320.5 48.8 %all-reduce.10.cloned.1.call-done = f32[1024,256]{1,0:T(8,128)} async-done(((f32[1024,256]{1,0:T(8,128)}), f32[1024,256]{1,0:T(8,128)}) %all-reduce.10.cloned.1.call-update) | async-done | bytes 1048592 | tf_op jit(solution)/shard_map/psum | solution.py:26
  369.3 1.3 broadcast_select_fusion
  371.8 28.4 %all-gather.17.cloned.1.call-done = f32[1024,256]{1,0:T(8,128)} async-done(((f32[256,256]{1,0:T(8,128)}), f32[1024,256]{1,0:T(8,128)}) %all-gather.17.cloned.1.call-update) | async-done | bytes 1048592 | tf_op jit(solution)/shard_map/all_gather | solution.py:31
  400.1 10.1 %fusion.15 = f32[1024,256]{1,0:T(8,128)} fusion(f32[1024,1024]{0,1:T(8,128)} %all-gather.13.cloned.1.call-done, f32[1024,256]{1,0:T(8,128)} %all-gather.17.cloned.1.call-done), kind=kOutput, calls=%fused_computation.39 | convolution fusion | flops 3221225472 | bytes 6291456 | tf_op jit(solution)/shard_map/dot_general | solution.py:38
  410.3 50.6 %all-reduce.12.cloned.1.call-done = f32[1024,256]{1,0:T(8,128)} async-done(((f32[1024,256]{1,0:T(8,128)}), f32[1024,256]{1,0:T(8,128)}) %all-reduce.12.cloned.1.call-update) | async-done | bytes 1048592 | tf_op jit(solution)/shard_map/psum | solution.py:26
  460.9 3.2 fusion
  464.1 128.6 %all-reduce = (f32[1]{0:T(128)}, f32[1]{0:T(128)}) all-reduce(f32[1]{0:T(128)} %bitcast.13, f32[1]{0:T(128)} %bitcast.12), channel_id=1, replica_groups=mesh['row'=4,'col'=16,'layer'=4] {'row','col'}, use_global_device_ids=true, to_apply=%region_7.8 | all-reduce | flops 2 | bytes 16 | tf_op jit(solution)/shard_map/psum | solution.py:75
  592.7 1.8 pad_maximum_fusion
  (34 shorter events, 3.8 us)
Async XLA Ops:
  7.2 32.2 %all-gather.9.cloned.1.call-start = ((), (), s32[]{:S(2)}) async-start(), calls=%async_computation.1 | async-start | bytes 1310720 | tf_op jit(solution)/shard_map/all_gather | solution.py:31
  8.9 75.3 %all-gather.7.cloned.1.call-start = ((), (), s32[]{:S(2)}) async-start(), calls=%async_computation | async-start | bytes 4456448 | tf_op jit(solution)/shard_map/all_gather | solution.py:39
  10.6 132.6 %copy-start.2 = (s32[64,64]{1,0:T(8,128)S(1)}, s32[64,64]{1,0:T(8,128)}, u32[]{:S(2)}) copy-start(s32[64,64]{1,0:T(8,128)} %param.3) | copy-start | bytes 49156
  11.3 131.9 %all-reduce.6.cloned.1.call-start = ((), (), s32[]{:S(2)}) async-start(), calls=%async_computation.2 | async-start | bytes 2097152 | tf_op jit(solution)/shard_map/psum | solution.py:26
  94.4 79.8 %all-gather.11.cloned.1.call-start = ((), (), s32[]{:S(2)}) async-start(), calls=%async_computation.3 | async-start | bytes 1310720 | tf_op jit(solution)/shard_map/all_gather | solution.py:31
  145.0 89.9 %copy-start.1 = (f32[1024,256]{1,0:T(8,128)S(1)}, f32[1024,256]{1,0:T(8,128)}, u32[]{:S(2)}) copy-start(f32[1024,256]{1,0:T(8,128)} %all-reduce.6.cloned.1.call-done) | copy-start | bytes 3145732
  145.7 89.1 %all-reduce.8.cloned.1.call-start = ((), (), s32[]{:S(2)}) async-start(), calls=%async_computation.4 | async-start | bytes 2097152 | tf_op jit(solution)/shard_map/psum | solution.py:26
  184.3 81.2 %all-gather.15.cloned.1.call-start = ((), (), s32[]{:S(2)}) async-start(), calls=%async_computation.6 | async-start | bytes 1310720 | tf_op jit(solution)/shard_map/all_gather | solution.py:31
  237.1 73.2 %all-gather.13.cloned.1.call-start = ((), (), s32[]{:S(2)}) async-start(), calls=%async_computation.5 | async-start | bytes 4456448 | tf_op jit(solution)/shard_map/all_gather | solution.py:39
  238.2 131.1 %all-reduce.10.cloned.1.call-start = ((), (), s32[]{:S(2)}) async-start(), calls=%async_computation.7 | async-start | bytes 2097152 | tf_op jit(solution)/shard_map/psum | solution.py:26
  320.5 79.6 %all-gather.17.cloned.1.call-start = ((), (), s32[]{:S(2)}) async-start(), calls=%async_computation.8 | async-start | bytes 1310720 | tf_op jit(solution)/shard_map/all_gather | solution.py:31
  370.7 90.2 %copy-start = (f32[1024,256]{1,0:T(8,128)S(1)}, f32[1024,256]{1,0:T(8,128)}, u32[]{:S(2)}) copy-start(f32[1024,256]{1,0:T(8,128)} %all-reduce.10.cloned.1.call-done) | copy-start | bytes 3145732
  371.4 89.4 %all-reduce.12.cloned.1.call-start = ((), (), s32[]{:S(2)}) async-start(), calls=%async_computation.9 | async-start | bytes 2097152 | tf_op jit(solution)/shard_map/psum | solution.py:26
Sparse Core Ops, SparseCore 0:
  9.8 29.4 all-gather.8
  41.7 42.4 all-gather.6
  94.5 48.6 all-reduce.5
  145.8 28.2 all-gather.10
  184.4 50.4 all-reduce.7
  237.2 28.2 all-gather.14
  267.9 42.4 all-gather.12
  320.6 48.6 all-reduce.9
  371.9 28.2 all-gather.16
  410.4 50.4 all-reduce.11
where the time goes:
time: 602 us; the launch traced here: 601 us
  waiting for transfers between devices  400 us (66%)
  blocking collectives  129 us (21%)
  matrix products  42.3 us (7%)
  between operations  14.3 us (2%)
  other arithmetic  7.89 us (1%)
  local copies, waits for them, and re-layouts  7.27 us (1%)
    psum x4, waiting for transfers between devices, reduce_layers(): summed = lax.psum(layer_term, 'layer')  199 us
    psum x1, blocking collectives, body(): trace_list.append(lax.psum(diag_part, ('row', 'col')))  129 us
    all_gather x4, waiting for transfers between devices, right_panel(): lax.all_gather(pick_rows(right, layer_index, unit_width, layers), 'row',...  111 us
    all_gather x2, waiting for transfers between devices, folded_product(): lax.all_gather(pick_columns(left, layer_index, unit_width, layers), 'col'...  89.7 us
    dot_general x4, matrix products, folded_product(): jnp.dot(lax.all_gather(pick_columns(left, layer_index, unit_width, layers...  40.5 us
  transfers between devices with their start and end apart: 10, of which 10 were waited for; matrix products, arithmetic and copies ran while one was open for 1% of the time, Pallas kernels for 0%

commit v1 on v0

--- a/solution.py
+++ b/solution.py
@@ -28,8 +28,14 @@
 
 
 def right_panel(right, layer_index, unit_width, layers):
-    return lax.all_gather(
-        pick_rows(right, layer_index, unit_width, layers), "row", axis=0, tiled=True
+    return jnp.concatenate(
+        lax.all_to_all(
+            jnp.stack([pick_rows(right, layer_index, unit_width, layers)] * lax.axis_size("row")),
+            "row",
+            0,
+            0,
+        ),
+        axis=0,
     )
 
 

time: 602 us -> 517 us (0.86)
  waiting for transfers between devices: 400 us -> 247 us
  blocking collectives: 129 us -> 202 us
    all_gather x4 -> x0, waiting for transfers between devices: 111 us -> none  [right_panel(): lax.all_gather(pick_rows(right, layer_index, unit_width, layers), 'row',...]
    all_to_all x0 -> x4, blocking collectives: none -> 73.8 us  [right_panel(): lax.all_to_all(jnp.stack([pick_rows(right, layer_index, unit_width, layer...]
    all_gather x2, waiting for transfers between devices: 89.7 us -> 51.6 us  [folded_product(): lax.all_gather(pick_columns(left, layer_index, unit_width, layers), 'col'...]
  transfers between devices with their start and end apart: 10 -> 6, of which waited for: 10 -> 6; matrix products, arithmetic and copies ran while one was open for 1% -> 0% of each run, Pallas kernels for 0% -> 0%
where the time goes in v1:
time: 517 us; the launch traced here: 516 us
  waiting for transfers between devices  247 us (48%)
  blocking collectives  202 us (39%)
  matrix products  39.2 us (8%)
  between operations  14.2 us (3%)
  other arithmetic  8 us (2%)
    psum x4, waiting for transfers between devices, reduce_layers(): summed = lax.psum(layer_term, 'layer')  196 us
    psum x1, blocking collectives, body(): trace_list.append(lax.psum(diag_part, ('row', 'col')))  129 us
    all_to_all x4, blocking collectives, right_panel(): lax.all_to_all(jnp.stack([pick_rows(right, layer_index, unit_width, layer...  73.8 us
    all_gather x2, waiting for transfers between devices, folded_product(): lax.all_gather(pick_columns(left, layer_index, unit_width, layers), 'col'...  51.6 us
    dot_general x4, matrix products, folded_product(): jnp.dot(lax.all_gather(pick_columns(left, layer_index, unit_width, layers...  37.4 us
  transfers between devices with their start and end apart: 6, of which 6 were waited for; matrix products, arithmetic and copies ran while one was open for 0% of the time, Pallas kernels for 0%

profile of v1, /device:TPU:2, one launch (start us, length us, event | category | flops | bytes accessed | tf_op | source)
XLA Modules:
  0.0 516.2 jit_solution(11720555575758756446)
XLA Ops:
  7.2 1.6 copy.4
  8.8 0.7 constant_dynamic-slice_fusion.5
  9.6 1.0 constant_dynamic-slice_fusion.4
  10.7 19.4 %all_to_all.20 = f32[4,256,256]{2,1,0:T(8,128)S(1)} all-to-all(f32[4,256,256]{2,1,0:T(8,128)S(1)} %stack.21), channel_id=1, replica_groups=mesh['row'=4,'col'=16,'layer'=4] {'row'}, dimensions={0} | all-to-all | bytes 2097152 | tf_op jit(solution)/shard_map/all_to_all | solution.py:32
  30.0 25.7 %all-gather.3.cloned.1.call-done = f32[1024,1024]{0,1:T(8,128)} async-done(((f32[1024,64]{0,1:T(8,128)}), f32[1024,1024]{0,1:T(8,128)}) %all-gather.3.cloned.1.call-update) | async-done | bytes 4194320 | tf_op jit(solution)/shard_map/all_gather | solution.py:45
  55.8 9.8 %fusion.12 = f32[1024,256]{1,0:T(8,128)} fusion(f32[1024,1024]{0,1:T(8,128)} %all-gather.3.cloned.1.call-done, f32[1024,256]{1,0:T(8,128)S(1)} %bitcast.27), kind=kOutput, calls=%fused_computation.36 | convolution fusion | flops 3221225472 | bytes 6291456 | tf_op jit(solution)/shard_map/dot_general | solution.py:44
  65.7 48.5 %all-reduce.6.cloned.1.call-done = f32[1024,256]{1,0:T(8,128)} async-done(((f32[1024,256]{1,0:T(8,128)}), f32[1024,256]{1,0:T(8,128)}) %all-reduce.6.cloned.1.call-update) | async-done | bytes 1048592 | tf_op jit(solution)/shard_map/psum | solution.py:26
  114.2 1.8 broadcast_select_fusion.1
  116.1 18.1 %all_to_all.21 = f32[4,256,256]{2,1,0:T(8,128)S(1)} all-to-all(f32[4,256,256]{2,1,0:T(8,128)S(1)} %stack.22), channel_id=1, replica_groups=mesh['row'=4,'col'=16,'layer'=4] {'row'}, dimensions={0} | all-to-all | bytes 2097152 | tf_op jit(solution)/shard_map/all_to_all | solution.py:32
  134.2 9.9 %fusion.13 = f32[1024,256]{1,0:T(8,128)} fusion(f32[1024,1024]{0,1:T(8,128)} %all-gather.3.cloned.1.call-done, f32[1024,256]{1,0:T(8,128)S(1)} %bitcast.29), kind=kOutput, calls=%fused_computation.37 | convolution fusion | flops 3221225472 | bytes 6291456 | tf_op jit(solution)/shard_map/dot_general | solution.py:44
  144.2 49.4 %all-reduce.8.cloned.1.call-done = f32[1024,256]{1,0:T(8,128)} async-done(((f32[1024,256]{1,0:T(8,128)}), f32[1024,256]{1,0:T(8,128)}) %all-reduce.8.cloned.1.call-update) | async-done | bytes 1048592 | tf_op jit(solution)/shard_map/psum | solution.py:26
  193.6 1.5 multiply_subtract_fusion.1
  195.4 0.7 constant_dynamic-slice_fusion.2
  196.3 18.1 %all_to_all.22 = f32[4,256,256]{2,1,0:T(8,128)S(1)} all-to-all(f32[4,256,256]{2,1,0:T(8,128)S(1)} %stack.23), channel_id=1, replica_groups=mesh['row'=4,'col'=16,'layer'=4] {'row'}, dimensions={0} | all-to-all | bytes 2097152 | tf_op jit(solution)/shard_map/all_to_all | solution.py:32
  214.4 25.9 %all-gather.5.cloned.1.call-done = f32[1024,1024]{0,1:T(8,128)} async-done(((f32[1024,64]{0,1:T(8,128)}), f32[1024,1024]{0,1:T(8,128)}) %all-gather.5.cloned.1.call-update) | async-done | bytes 4194320 | tf_op jit(solution)/shard_map/all_gather | solution.py:45
  240.3 9.8 %fusion.14 = f32[1024,256]{1,0:T(8,128)} fusion(f32[1024,1024]{0,1:T(8,128)} %all-gather.5.cloned.1.call-done, f32[1024,256]{1,0:T(8,128)S(1)} %bitcast.28), kind=kOutput, calls=%fused_computation.38 | convolution fusion | flops 3221225472 | bytes 6291456 | tf_op jit(solution)/shard_map/dot_general | solution.py:44
  250.2 48.5 %all-reduce.10.cloned.1.call-done = f32[1024,256]{1,0:T(8,128)} async-done(((f32[1024,256]{1,0:T(8,128)}), f32[1024,256]{1,0:T(8,128)}) %all-reduce.10.cloned.1.call-update) | async-done | bytes 1048592 | tf_op jit(solution)/shard_map/psum | solution.py:26
  298.8 1.5 broadcast_select_fusion
  300.4 18.1 %all_to_all.23 = f32[4,256,256]{2,1,0:T(8,128)S(1)} all-to-all(f32[4,256,256]{2,1,0:T(8,128)S(1)} %stack.24), channel_id=1, replica_groups=mesh['row'=4,'col'=16,'layer'=4] {'row'}, dimensions={0} | all-to-all | bytes 2097152 | tf_op jit(solution)/shard_map/all_to_all | solution.py:32
  318.5 7.8 %fusion.15 = f32[1024,256]{1,0:T(8,128)} fusion(f32[1024,1024]{0,1:T(8,128)S(1)} %copy-done, f32[1024,256]{1,0:T(8,128)S(1)} %bitcast.30), kind=kOutput, calls=%fused_computation.39 | convolution fusion | flops 3221225472 | bytes 6291456 | tf_op jit(solution)/shard_map/dot_general | solution.py:44
  326.4 49.4 %all-reduce.12.cloned.1.call-done = f32[1024,256]{1,0:T(8,128)} async-done(((f32[1024,256]{1,0:T(8,128)}), f32[1024,256]{1,0:T(8,128)}) %all-reduce.12.cloned.1.call-update) | async-done | bytes 1048592 | tf_op jit(solution)/shard_map/psum | solution.py:26
  375.8 3.2 fusion
  379.0 128.6 %all-reduce = (f32[1]{0:T(128)}, f32[1]{0:T(128)}) all-reduce(f32[1]{0:T(128)} %bitcast.17, f32[1]{0:T(128)} %bitcast.16), channel_id=1, replica_groups=mesh['row'=4,'col'=16,'layer'=4] {'row','col'}, use_global_device_ids=true, to_apply=%region_7.8 | all-reduce | flops 2 | bytes 16 | tf_op jit(solution)/shard_map/psum | solution.py:81
  507.6 1.8 pad_maximum_fusion
  (32 shorter events, 1.1 us)
Async XLA Ops:
  7.2 48.6 %all-gather.3.cloned.1.call-start = ((), (), s32[]{:S(2)}) async-start(), calls=%async_computation.4 | async-start | bytes 4456448 | tf_op jit(solution)/shard_map/all_gather | solution.py:45
  9.5 104.6 %all-reduce.6.cloned.1.call-start = ((), (), s32[]{:S(2)}) async-start(), calls=%async_computation.5 | async-start | bytes 2097152 | tf_op jit(solution)/shard_map/psum | solution.py:26
  30.0 84.2 %copy-start.3 = (s32[64,64]{1,0:T(8,128)S(1)}, s32[64,64]{1,0:T(8,128)}, u32[]{:S(2)}) copy-start(s32[64,64]{1,0:T(8,128)} %param.3) | copy-start | bytes 49156
  65.6 128.0 %all-reduce.8.cloned.1.call-start = ((), (), s32[]{:S(2)}) async-start(), calls=%async_computation.6 | async-start | bytes 2097152 | tf_op jit(solution)/shard_map/psum | solution.py:26
  134.2 59.4 %copy-start.2 = (f32[1024,256]{1,0:T(8,128)S(1)}, f32[1024,256]{1,0:T(8,128)}, u32[]{:S(2)}) copy-start(f32[1024,256]{1,0:T(8,128)} %all-reduce.6.cloned.1.call-done) | copy-start | bytes 3145732
  144.2 96.2 %all-gather.5.cloned.1.call-start = ((), (), s32[]{:S(2)}) async-start(), calls=%async_computation.7 | async-start | bytes 4456448 | tf_op jit(solution)/shard_map/all_gather | solution.py:45
  196.1 102.6 %all-reduce.10.cloned.1.call-start = ((), (), s32[]{:S(2)}) async-start(), calls=%async_computation.8 | async-start | bytes 2097152 | tf_op jit(solution)/shard_map/psum | solution.py:26
  250.2 125.6 %all-reduce.12.cloned.1.call-start = ((), (), s32[]{:S(2)}) async-start(), calls=%async_computation.9 | async-start | bytes 2097152 | tf_op jit(solution)/shard_map/psum | solution.py:26
  298.8 19.8 %copy-start = (f32[1024,1024]{0,1:T(8,128)S(1)}, f32[1024,1024]{0,1:T(8,128)}, u32[]{:S(2)}) copy-start(f32[1024,1024]{0,1:T(8,128)} %all-gather.5.cloned.1.call-done) | copy-start | bytes 12582916
  318.5 57.3 %copy-start.1 = (f32[1024,256]{1,0:T(8,128)S(1)}, f32[1024,256]{1,0:T(8,128)}, u32[]{:S(2)}) copy-start(f32[1024,256]{1,0:T(8,128)} %all-reduce.10.cloned.1.call-done) | copy-start | bytes 3145732
Sparse Core Ops, SparseCore 0:
  10.4 45.3 all-gather.2
  65.7 48.3 all-reduce.5
  144.3 49.2 all-reduce.7
  196.3 44.0 all-gather.4
  250.3 48.3 all-reduce.9
  326.5 49.2 all-reduce.11
